TPU v7x, 512 devices: a whole 4x4x16 slice. The times are simulated.
512 devices in a mesh: row: 32 (over y, x, core), col: 16 (over z).
Axes of the slice: x: 4, y: 4, z: 16, core: 2. Of those that a mesh axis runs over, the one named last changes fastest.
Arguments:
- matrix: float32 [12288, 12288], P('row', 'col'), may hold values from -10 to 10, as said below
- panel: float32 [12288, 64], P('row'), may hold values from -1.12763724 to 1.12763724
Outputs:
- updated: float32 [12288, 12288], P('row', 'col')
- band_block: float32 [64, 64], replicated
Inputs may be any that keep to these rules, and one draw needn't show every extreme that they name: matrix is exactly symmetric.
All inputs are finite; a program needn't handle non-finite values.
Results may differ from a plain program's by a relative error of at most 0.0002.
Values sent between devices are 32-bit elements; how exact they have to be, the bound alone decides.
A program may use at most 64 MiB of HBM per device.

v0:
```python
import jax
import jax.numpy as jnp
from jax import lax
from jax.sharding import PartitionSpec as P

precise = lax.Precision.HIGHEST


def partner_2(block, axis, stride):
    count = lax.axis_size(axis)
    route = []
    for low in range(count):
        high = low | 1 << stride
        if high != low and high < count:
            route += [(low, high), (high, low)]
    return lax.ppermute(block, axis, route)


def from_root(value, axis, source):
    kept = jnp.where(lax.axis_index(axis) == source, value, 0).astype(value.dtype)
    return lax.psum(kept, axis)


def upper_cholesky(gram_block):
    order_now = gram_block.shape[0]
    positions = jnp.arange(order_now)

    def one_column(column_index, lower_part):
        gram_column = lax.dynamic_slice_in_dim(gram_block, column_index, 1, 1)[:, 0]
        lower_row = lax.dynamic_slice_in_dim(lower_part, column_index, 1, 0)[0]
        earlier = jnp.where(positions < column_index, lower_row, 0.0)
        reduced = gram_column - jnp.dot(lower_part, earlier, precision=precise)
        pivot_value = jnp.sum(jnp.where(positions == column_index, reduced, 0.0))
        diagonal_value = jnp.sqrt(pivot_value)
        new_column = jnp.where(positions > column_index, reduced / diagonal_value, 0.0) + jnp.where(
            positions == column_index, diagonal_value, 0.0
        )
        return jnp.where(positions[None, :] == column_index, new_column[:, None], lower_part)

    lower_part = lax.fori_loop(
        0, order_now, one_column, jnp.zeros((order_now, order_now), jnp.float32)
    )
    return lower_part.T


def upper_inverse(upper_block):
    order_now = upper_block.shape[0]
    positions = jnp.arange(order_now)

    def one_row(step_count, inverse_part):
        row_at = order_now - 1 - step_count
        upper_row = lax.dynamic_slice_in_dim(upper_block, row_at, 1, 0)[0]
        diagonal_value = jnp.sum(jnp.where(positions == row_at, upper_row, 0.0))
        beyond = jnp.where(positions > row_at, upper_row, 0.0)
        unit_row = jnp.where(positions == row_at, 1.0, 0.0)
        new_row = (unit_row - jnp.dot(beyond, inverse_part, precision=precise)) / diagonal_value
        return jnp.where(positions[:, None] == row_at, new_row[None, :], inverse_part)

    return lax.fori_loop(0, order_now, one_row, jnp.zeros((order_now, order_now), jnp.float32))


def small_factor(block_in):
    order_now = block_in.shape[0]
    positions = jnp.arange(order_now)

    def one_pivot(pivot_index, state_pair):
        working, lower_whole = state_pair
        pivot_column = lax.dynamic_slice_in_dim(working, pivot_index, 1, 1)[:, 0]
        pivot_row = lax.dynamic_slice_in_dim(working, pivot_index, 1, 0)[0]
        pivot_value = jnp.sum(jnp.where(positions == pivot_index, pivot_column, 0.0))
        multipliers = jnp.where(positions > pivot_index, pivot_column / pivot_value, 0.0)
        lower_whole = lower_whole + multipliers[:, None] * (
            positions[None, :] == pivot_index
        ).astype(jnp.float32)
        working = working - multipliers[:, None] * pivot_row[None, :]
        return (working, lower_whole)

    working, lower_whole = lax.fori_loop(
        0, order_now, one_pivot, (block_in, jnp.eye(order_now, dtype=jnp.float32))
    )
    return (lower_whole, jnp.triu(working))


def body(matrix, panel):
    local_rows, local_columns = matrix.shape
    panel_width = panel.shape[1]
    row_index = lax.axis_index("row")
    current_column_index = lax.axis_index("col")
    local_inner = jnp.dot(panel.T, panel, precision=precise)
    head_rows = panel[:panel_width]
    band_factor = -upper_cholesky(local_inner)
    levels = lax.axis_size("row").bit_length() - 1
    for bit_level in range(levels):
        partner = partner_2(band_factor, "row", bit_level)
        keeps_first = row_index >> bit_level & 1 == 0
        earlier_one = jnp.where(keeps_first, band_factor, partner)
        later_one = jnp.where(keeps_first, partner, band_factor)
        paired = jnp.dot(earlier_one.T, earlier_one, precision=precise) + jnp.dot(
            later_one.T, later_one, precision=precise
        )
        band_factor = -upper_cholesky(paired)
    head_rows = from_root(head_rows, "row", 0)
    factor_inverse = upper_inverse(band_factor)
    orthogonal_rows = jnp.dot(panel, factor_inverse, precision=precise)
    orthogonal_head = jnp.dot(head_rows, factor_inverse, precision=precise)
    identity = jnp.eye(panel_width, dtype=jnp.float32)
    lower_whole, upper_whole = small_factor(orthogonal_head - identity)
    global_rows = row_index * local_rows + jnp.arange(local_rows)
    unit_rows = (global_rows[:, None] == jnp.arange(panel_width)[None, :]).astype(jnp.float32)
    reflect_rows = jnp.dot(
        orthogonal_rows - unit_rows, upper_inverse(upper_whole), precision=precise
    )
    triangle = -jnp.dot(upper_whole, upper_inverse(lower_whole.T), precision=precise)
    gathered_reflect = lax.all_gather(reflect_rows, "row", axis=0, tiled=True)
    reflect_columns = lax.dynamic_slice_in_dim(
        gathered_reflect, current_column_index * local_columns, local_columns, 0
    )
    partial_product = lax.dot_general(
        matrix, reflect_rows, (((0,), (0,)), ((), ())), precision=precise
    )
    product = lax.psum(partial_product, "row")
    applied_cols = jnp.dot(product, triangle, precision=precise)
    inner_part = jnp.dot(reflect_columns.T, applied_cols, precision=precise)
    inner_total = lax.psum(inner_part, "col")
    coupling = jnp.dot(triangle.T, inner_total, precision=precise)
    corrected_cols = applied_cols - 0.5 * jnp.dot(reflect_columns, coupling, precision=precise)
    gathered_corrected = lax.all_gather(corrected_cols, "col", axis=0, tiled=True)
    corrected_rows = lax.dynamic_slice_in_dim(
        gathered_corrected, row_index * local_rows, local_rows, 0
    )
    left_factor = jnp.concatenate([reflect_rows, corrected_rows], 1)
    right_factor = jnp.concatenate([corrected_cols, reflect_columns], 1)
    updated = matrix - lax.dot_general(
        left_factor, right_factor, (((1,), (1,)), ((), ())), precision=precise
    )
    return (updated, band_factor)


def solution(mesh):
    return jax.shard_map(
        body,
        mesh=mesh,
        in_specs=(P("row", "col"), P("row", None)),
        out_specs=(P("row", "col"), P()),
        check_vma=False,
    )
```

profile of v0, /device:TPU:14, one launch (start us, length us, event | category | flops | bytes accessed | tf_op | source)
XLA Modules:
  0.0 1399.8 jit_solution(851780001571916975)
XLA Ops:
  7.2 1.2 fusion.154
  8.5 101.3 %while.159 = (s32[]{:T(128)}, f32[64,64]{1,0:T(8,128)S(1)}, f32[64,64]{0,1:T(8,128)S(1)}, s32[]{:T(128)}, s32[]{:T(128)}) while((s32[]{:T(128)}, f32[64,64]{1,0:T(8,128)S(1)}, f32[64,64]{0,1:T(8,128)S(1)}, s32[]{:T(128)}, s32[]{:T(128)}) %tuple.367), condition=%wide.region_2.3_spmd.clone.clone, body=%wide.region_0.2_spmd.clone.clone.sunk | while | flops 62274 | bytes 102632 | solution.py:40
  109.8 1.9 collective-permute-start
  111.9 1.1 collective-permute-done
  113.4 101.3 %while.160 = (s32[]{:T(128)}, f32[64,64]{1,0:T(8,128)S(1)}, f32[64,64]{0,1:T(8,128)S(1)}, s32[]{:T(128)}, s32[]{:T(128)}) while((s32[]{:T(128)}, f32[64,64]{1,0:T(8,128)S(1)}, f32[64,64]{0,1:T(8,128)S(1)}, s32[]{:T(128)}, s32[]{:T(128)}) %tuple.370), condition=%wide.region_5.6_spmd.clone.clone, body=%wide.region_3.5_spmd.clone.clone.sunk | while | flops 62274 | bytes 102632 | solution.py:40
  214.7 2.7 collective-permute-start.1
  217.5 3.0 collective-permute-done.1
  220.9 101.3 %while.161 = (s32[]{:T(128)}, f32[64,64]{1,0:T(8,128)S(1)}, f32[64,64]{0,1:T(8,128)S(1)}, s32[]{:T(128)}, s32[]{:T(128)}) while((s32[]{:T(128)}, f32[64,64]{1,0:T(8,128)S(1)}, f32[64,64]{0,1:T(8,128)S(1)}, s32[]{:T(128)}, s32[]{:T(128)}) %tuple.373), condition=%wide.region_8.9_spmd.clone.clone, body=%wide.region_6.8_spmd.clone.clone.sunk | while | flops 62274 | bytes 102632 | solution.py:40
  322.3 3.3 collective-permute-start.2
  325.6 4.0 collective-permute-done.2
  330.1 101.3 %while.162 = (s32[]{:T(128)}, f32[64,64]{1,0:T(8,128)S(1)}, f32[64,64]{0,1:T(8,128)S(1)}, s32[]{:T(128)}, s32[]{:T(128)}) while((s32[]{:T(128)}, f32[64,64]{1,0:T(8,128)S(1)}, f32[64,64]{0,1:T(8,128)S(1)}, s32[]{:T(128)}, s32[]{:T(128)}) %tuple.376), condition=%wide.region_11.12_spmd.clone.clone, body=%wide.region_9.11_spmd.clone.clone.sunk | while | flops 62274 | bytes 102632 | solution.py:40
  431.4 4.1 collective-permute-start.3
  435.5 1.8 collective-permute-done.3
  437.9 101.3 %while.163 = (s32[]{:T(128)}, f32[64,64]{1,0:T(8,128)S(1)}, f32[64,64]{0,1:T(8,128)S(1)}, s32[]{:T(128)}, s32[]{:T(128)}) while((s32[]{:T(128)}, f32[64,64]{1,0:T(8,128)S(1)}, f32[64,64]{0,1:T(8,128)S(1)}, s32[]{:T(128)}, s32[]{:T(128)}) %tuple.379), condition=%wide.region_14.15_spmd.clone.clone, body=%wide.region_12.14_spmd.clone.clone.sunk | while | flops 62274 | bytes 102632 | solution.py:40
  539.2 4.0 collective-permute-start.4
  543.3 102.9 %psum.21 = f32[64,64]{1,0:T(8,128)S(1)} all-reduce(f32[64,64]{1,0:T(8,128)S(1)} %broadcast_select_fusion.12), channel_id=1, replica_groups=mesh['row'=32,'col'=16] {'row'}, use_global_device_ids=true, to_apply=%region_21.22 | all-reduce | flops 4096 | bytes 32768 | tf_op jit(solution)/shard_map/psum | solution.py:21
  646.6 102.2 %while.164 = (s32[]{:T(128)}, f32[64,64]{1,0:T(8,128)S(1)}, f32[64,64]{0,1:T(8,128)S(1)}, s32[]{:T(128)}, s32[]{:T(128)}) while((s32[]{:T(128)}, f32[64,64]{1,0:T(8,128)S(1)}, f32[64,64]{0,1:T(8,128)S(1)}, s32[]{:T(128)}, s32[]{:T(128)}) %tuple.382), condition=%wide.region_17.18_spmd.clone.clone, body=%wide.region_15.17_spmd.clone.clone.sunk | while | flops 62274 | bytes 102632 | solution.py:40
  749.0 95.1 %while.165 = (s32[]{:T(128)}, f32[64,64]{1,0:T(8,128)S(1)}, f32[64,64]{1,0:T(8,128)S(1)}, s32[]{:T(128)}, s32[]{:T(128)}, /*index=5*/s32[]{:T(128)}, s32[]{:T(128)}) while((s32[]{:T(128)}, f32[64,64]{1,0:T(8,128)S(1)}, f32[64,64]{1,0:T(8,128)S(1)}, s32[]{:T(128)}, s32[]{:T(128)}, /*index=5*/s32[]{:T(128)}, ...), condition=%wide.region_20.21_spmd.clone.clone, body=%wide.region_18.20_spmd.clone.clone.sunk | while | flops 62086 | bytes 69153 | solution.py:59
  844.3 100.7 %while.158 = (s32[]{:T(128)}, f32[64,64]{0,1:T(8,128)S(1)}, f32[64,64]{0,1:T(8,128)S(1)}, s32[]{:T(128)}) while((s32[]{:T(128)}, f32[64,64]{0,1:T(8,128)S(1)}, f32[64,64]{0,1:T(8,128)S(1)}, s32[]{:T(128)}) %tuple.388), condition=%wide.region_24.25_spmd.clone.clone, body=%wide.region_22.24_spmd.clone.clone.sunk | while | flops 16897 | bytes 69965 | solution.py:78
  945.1 95.1 %while.166 = (s32[]{:T(128)}, f32[64,64]{1,0:T(8,128)S(1)}, f32[64,64]{1,0:T(8,128)S(1)}, s32[]{:T(128)}, s32[]{:T(128)}, /*index=5*/s32[]{:T(128)}, s32[]{:T(128)}) while((s32[]{:T(128)}, f32[64,64]{1,0:T(8,128)S(1)}, f32[64,64]{1,0:T(8,128)S(1)}, s32[]{:T(128)}, s32[]{:T(128)}, /*index=5*/s32[]{:T(128)}, ...), condition=%wide.region_27.28_spmd.clone.clone, body=%wide.region_25.27_spmd.clone.clone.sunk | while | flops 62086 | bytes 69153 | solution.py:59
  1040.8 1.5 convolution_bitcast_fusion.9
  1043.2 103.2 %while.167 = (s32[]{:T(128)}, f32[64,64]{1,0:T(8,128)S(1)}, f32[64,64]{1,0:T(8,128)S(1)}, s32[]{:T(128)}, s32[]{:T(128)}, /*index=5*/s32[]{:T(128)}, s32[]{:T(128)}) while((s32[]{:T(128)}, f32[64,64]{1,0:T(8,128)S(1)}, f32[64,64]{1,0:T(8,128)S(1)}, s32[]{:T(128)}, s32[]{:T(128)}, /*index=5*/s32[]{:T(128)}, ...), condition=%wide.region_31.32_spmd.clone.clone, body=%wide.region_29.31_spmd.clone.clone.sunk | while | flops 62086 | bytes 69153 | solution.py:59
  1058.4 0.8 fusion.236
  1060.0 0.8 fusion.236
  1061.6 0.8 fusion.236
  1063.2 0.8 fusion.236
  1064.8 0.8 fusion.236
  1066.4 0.8 fusion.236
  1068.1 0.8 fusion.236
  1082.6 0.8 fusion.236
  1098.7 0.8 fusion.236
  1100.3 0.8 fusion.236
  1101.9 0.8 fusion.236
  1103.5 0.8 fusion.236
  1105.1 0.8 fusion.236
  1106.7 0.8 fusion.236
  1116.4 0.8 fusion.236
  1119.6 0.8 fusion.236
  1143.8 0.8 fusion.236
  1146.5 45.9 %all-reduce.2.cloned.1.call-done = f32[768,64]{0,1:T(8,128)} async-done(((f32[768,64]{0,1:T(8,128)}), f32[768,64]{0,1:T(8,128)}) %all-reduce.2.cloned.1.call-update) | async-done | bytes 196624 | tf_op jit(solution)/shard_map/psum | solution.py:121
  1192.4 1.3 fusion.156
  1193.7 62.0 %all-gather.3.cloned.1.call-done = f32[12288,64]{0,1:T(8,128)} async-done(((f32[384,64]{0,1:T(8,128)}), f32[12288,64]{0,1:T(8,128)}) %all-gather.3.cloned.1.call-update) | async-done | bytes 3145744 | tf_op jit(solution)/shard_map/all_gather | solution.py:114
  1255.6 0.9 constant_dynamic-slice_fusion.8
  1256.9 56.9 %psum.23 = f32[64,64]{1,0:T(8,128)S(1)} all-reduce(f32[64,64]{1,0:T(8,128)S(1)} %fusion.157), channel_id=1, replica_groups=mesh['row'=32,'col'=16] {'col'}, use_global_device_ids=true, to_apply=%region_32.33 | all-reduce | flops 4096 | bytes 32768 | tf_op jit(solution)/shard_map/psum | solution.py:124
  1314.0 1.0 fusion.118
  1315.1 74.2 %all-gather.5.cloned.1.call-done = f32[12288,64]{0,1:T(8,128)} async-done(((f32[768,64]{0,1:T(8,128)}), f32[12288,64]{0,1:T(8,128)}) %all-gather.5.cloned.1.call-update) | async-done | bytes 3145744 | tf_op jit(solution)/shard_map/all_gather | solution.py:127
  1389.3 0.9 constant_dynamic-slice_fusion.7
  1390.2 3.1 convolution_subtract_fusion
  (3056 shorter events, 716.6 us)
Async XLA Ops:
  7.2 104.6 %slice-start = ((f32[384,64]{0,1:T(8,128)}), f32[64,64]{0,1:T(8,128)S(1)}, s32[]{:S(2)}) async-start(f32[384,64]{0,1:T(8,128)} %param.23), calls=%async_computation.3 | async-start | bytes 65536 | tf_op jit(solution)/shard_map/slice | solution.py:90
  7.2 1185.2 %all-reduce.2.cloned.1.call-start = ((), (), s32[]{:S(2)}) async-start(), calls=%async_computation | async-start | bytes 393216 | tf_op jit(solution)/shard_map/psum | solution.py:121
  109.8 3.1 collective-permute-start
  214.7 5.8 collective-permute-start.1
  322.3 7.3 collective-permute-start.2
  431.4 6.0 collective-permute-start.3
  539.2 107.0 %collective-permute-start.4 = (f32[64,64]{0,1:T(8,128)S(1)}, f32[64,64]{0,1:T(8,128)S(1)}, u32[]{:S(2)}, u32[]{:S(2)}) collective-permute-start(f32[64,64]{0,1:T(8,128)S(1)} %negate_bitcast_fusion.1), channel_id=1, source_target_pairs={{0,256},{256,0},{16,272},{272,16},{32,288},{288,32},{48,304},{304,... | collective-permute-start | bytes 49160 | tf_op jit(solution)/shard_map/ppermute | solution.py:16
  748.9 291.3 %copy-start.3 = (f32[384,64]{0,1:T(8,128)S(1)}, f32[384,64]{0,1:T(8,128)}, u32[]{:S(2)}) copy-start(f32[384,64]{0,1:T(8,128)} %param.23) | copy-start | bytes 294916
  749.0 291.9 %copy-start = (f32[384,768]{1,0:T(8,128)S(1)}, f32[384,768]{1,0:T(8,128)}, u32[]{:S(2)}) copy-start(f32[384,768]{1,0:T(8,128)} %param.22) | copy-start | bytes 3538948
  844.1 196.8 %copy-start.4 = (f32[64,64]{1,0:T(8,128)}, f32[64,64]{1,0:T(8,128)S(1)}, u32[]{:S(2)}) copy-start(f32[64,64]{1,0:T(8,128)S(1)} %get-tuple-element.1720) | copy-start | bytes 49156
  1040.8 1.6 copy-start.1
  1042.4 213.3 %all-gather.3.cloned.1.call-start = ((), (), s32[]{:S(2)}) async-start(), calls=%async_computation.1 | async-start | bytes 3244032 | tf_op jit(solution)/shard_map/all_gather | solution.py:114
  1043.1 346.2 %all-gather.5.cloned.1.call-start = ((), (), s32[]{:S(2)}) async-start(), calls=%async_computation.2 | async-start | bytes 3342336 | tf_op jit(solution)/shard_map/all_gather | solution.py:127
  1146.5 243.7 %copy-start.2 = (f32[384,64]{0,1:T(8,128)S(1)}, f32[384,64]{0,1:T(8,128)}, u32[]{:S(2)}) copy-start(f32[384,64]{0,1:T(8,128)} %copy-done.1) | copy-start | bytes 294916
Sparse Core Ops, SparseCore 0:
  1042.5 149.8 all-reduce.1
  1196.1 59.4 all-gather.2
  1315.2 74.0 all-gather.4
where the time goes:
time: 1410 us; the launch traced here: 1400 us
  matrix products  464 us (33%)
  loops' own time  277 us (20%)
  other arithmetic  262 us (19%)
  waiting for transfers between devices  193 us (14%)
  blocking collectives  160 us (11%)
  starting transfers between devices  16.2 us (1%)
  between operations  14.2 us (1%)
    dot_general x384, matrix products, one_column(): reduced = gram_column - jnp.dot(lower_part, earlier, precision=precise)  299 us
    another operation x6, loops' own time, upper_cholesky(): lax.fori_loop(0, order_now, one_column, jnp.zeros((order_now, order_now),...  274 us
    dot_general x192, matrix products, one_row(): jnp.dot(beyond, inverse_part, precision=precise)  154 us
    reduce_sum x192, other arithmetic, one_row(): diagonal_value = jnp.sum(jnp.where(positions == row_at, upper_row, 0.0))  123 us
    psum x1, blocking collectives, from_root(): return lax.psum(kept, axis)  103 us
    all_gather x1, waiting for transfers between devices, body(): lax.all_gather(corrected_cols, 'col', axis=0, tiled=True)  74.2 us
    all_gather x1, waiting for transfers between devices, body(): gathered_reflect = lax.all_gather(reflect_rows, 'row', axis=0, tiled=True)  62 us
    psum x1, blocking collectives, body(): inner_total = lax.psum(inner_part, 'col')  56.9 us
  transfers between devices with their start and end apart: 8, of which 7 were waited for; matrix products, arithmetic and copies ran while one was open for 7% of the time, Pallas kernels for 0%

commit v1 on v0

--- a/solution.py
+++ b/solution.py
@@ -124,7 +124,8 @@
     inner_total = lax.psum(inner_part, "col")
     coupling = jnp.dot(triangle.T, inner_total, precision=precise)
     corrected_cols = applied_cols - 0.5 * jnp.dot(reflect_columns, coupling, precision=precise)
-    gathered_corrected = lax.all_gather(corrected_cols, "col", axis=0, tiled=True)
+    sent = jnp.stack([corrected_cols] * lax.axis_size("col"))
+    gathered_corrected = jnp.concatenate(lax.all_to_all(sent, "col", 0, 0), axis=0)
     corrected_rows = lax.dynamic_slice_in_dim(
         gathered_corrected, row_index * local_rows, local_rows, 0
     )

time: 1410 us -> 1470 us (1.043)
  the two profiles are of different devices: /device:TPU:14 before, /device:TPU:32 now
where the time goes in v1:
time: 1470 us; the launch traced here: 1460 us
  matrix products  462 us (31%)
  loops' own time  277 us (19%)
  other arithmetic  262 us (18%)
  waiting for transfers between devices  221 us (15%)
  blocking collectives  179 us (12%)
  starting transfers between devices  29.3 us (2%)
  local copies, waits for them, and re-layouts  16.8 us (1%)
    dot_general x384, matrix products, one_column(): reduced = gram_column - jnp.dot(lower_part, earlier, precision=precise)  299 us
    another operation x6, loops' own time, upper_cholesky(): lax.fori_loop(0, order_now, one_column, jnp.zeros((order_now, order_now),...  274 us
    dot_general x192, matrix products, one_row(): jnp.dot(beyond, inverse_part, precision=precise)  154 us
    all_to_all x1, waiting for transfers between devices, body(): lax.all_to_all(sent, 'col', 0, 0)  125 us
    psum x1, blocking collectives, from_root(): return lax.psum(kept, axis)  124 us
    reduce_sum x192, other arithmetic, one_row(): diagonal_value = jnp.sum(jnp.where(positions == row_at, upper_row, 0.0))  123 us
    all_gather x1, waiting for transfers between devices, body(): gathered_reflect = lax.all_gather(reflect_rows, 'row', axis=0, tiled=True)  62.1 us
    psum x1, blocking collectives, body(): inner_total = lax.psum(inner_part, 'col')  55.5 us
  transfers between devices with their start and end apart: 8, of which 7 were waited for; matrix products, arithmetic and copies ran while one was open for 7% of the time, Pallas kernels for 0%

profile of v1, /device:TPU:32, one launch (start us, length us, event | category | flops | bytes accessed | tf_op | source)
XLA Modules:
  0.0 1462.9 jit_solution(9975379302553752711)
XLA Ops:
  7.2 1.2 fusion.154
  8.5 101.3 %while.159 = (s32[]{:T(128)}, f32[64,64]{1,0:T(8,128)S(1)}, f32[64,64]{0,1:T(8,128)S(1)}, s32[]{:T(128)}, s32[]{:T(128)}) while((s32[]{:T(128)}, f32[64,64]{1,0:T(8,128)S(1)}, f32[64,64]{0,1:T(8,128)S(1)}, s32[]{:T(128)}, s32[]{:T(128)}) %tuple.374), condition=%wide.region_2.3_spmd.clone.clone, body=%wide.region_0.2_spmd.clone.clone.sunk | while | flops 62274 | bytes 102632 | solution.py:40
  109.8 1.9 collective-permute-start
  111.9 1.1 collective-permute-done
  113.4 101.3 %while.160 = (s32[]{:T(128)}, f32[64,64]{1,0:T(8,128)S(1)}, f32[64,64]{0,1:T(8,128)S(1)}, s32[]{:T(128)}, s32[]{:T(128)}) while((s32[]{:T(128)}, f32[64,64]{1,0:T(8,128)S(1)}, f32[64,64]{0,1:T(8,128)S(1)}, s32[]{:T(128)}, s32[]{:T(128)}) %tuple.377), condition=%wide.region_5.6_spmd.clone.clone, body=%wide.region_3.5_spmd.clone.clone.sunk | while | flops 62274 | bytes 102632 | solution.py:40
  214.7 3.4 collective-permute-start.1
  218.1 2.4 collective-permute-done.1
  221.0 101.3 %while.161 = (s32[]{:T(128)}, f32[64,64]{1,0:T(8,128)S(1)}, f32[64,64]{0,1:T(8,128)S(1)}, s32[]{:T(128)}, s32[]{:T(128)}) while((s32[]{:T(128)}, f32[64,64]{1,0:T(8,128)S(1)}, f32[64,64]{0,1:T(8,128)S(1)}, s32[]{:T(128)}, s32[]{:T(128)}) %tuple.380), condition=%wide.region_8.9_spmd.clone.clone, body=%wide.region_6.8_spmd.clone.clone.sunk | while | flops 62274 | bytes 102632 | solution.py:40
  322.3 4.9 collective-permute-start.2
  327.3 2.3 collective-permute-done.2
  330.1 101.3 %while.162 = (s32[]{:T(128)}, f32[64,64]{1,0:T(8,128)S(1)}, f32[64,64]{0,1:T(8,128)S(1)}, s32[]{:T(128)}, s32[]{:T(128)}) while((s32[]{:T(128)}, f32[64,64]{1,0:T(8,128)S(1)}, f32[64,64]{0,1:T(8,128)S(1)}, s32[]{:T(128)}, s32[]{:T(128)}) %tuple.383), condition=%wide.region_11.12_spmd.clone.clone, body=%wide.region_9.11_spmd.clone.clone.sunk | while | flops 62274 | bytes 102632 | solution.py:40
  431.4 3.5 collective-permute-start.3
  434.9 2.3 collective-permute-done.3
  437.6 101.3 %while.163 = (s32[]{:T(128)}, f32[64,64]{1,0:T(8,128)S(1)}, f32[64,64]{0,1:T(8,128)S(1)}, s32[]{:T(128)}, s32[]{:T(128)}) while((s32[]{:T(128)}, f32[64,64]{1,0:T(8,128)S(1)}, f32[64,64]{0,1:T(8,128)S(1)}, s32[]{:T(128)}, s32[]{:T(128)}) %tuple.386), condition=%wide.region_14.15_spmd.clone.clone, body=%wide.region_12.14_spmd.clone.clone.sunk | while | flops 62274 | bytes 102632 | solution.py:40
  539.0 5.1 collective-permute-start.4
  544.2 123.8 %psum.21 = f32[64,64]{1,0:T(8,128)S(1)} all-reduce(f32[64,64]{1,0:T(8,128)S(1)} %broadcast_select_fusion.12), channel_id=1, replica_groups=mesh['row'=32,'col'=16] {'row'}, use_global_device_ids=true, to_apply=%region_21.22 | all-reduce | flops 4096 | bytes 32768 | tf_op jit(solution)/shard_map/psum | solution.py:21
  668.4 102.2 %while.164 = (s32[]{:T(128)}, f32[64,64]{1,0:T(8,128)S(1)}, f32[64,64]{0,1:T(8,128)S(1)}, s32[]{:T(128)}, s32[]{:T(128)}) while((s32[]{:T(128)}, f32[64,64]{1,0:T(8,128)S(1)}, f32[64,64]{0,1:T(8,128)S(1)}, s32[]{:T(128)}, s32[]{:T(128)}) %tuple.389), condition=%wide.region_17.18_spmd.clone.clone, body=%wide.region_15.17_spmd.clone.clone.sunk | while | flops 62274 | bytes 102632 | solution.py:40
  770.8 95.1 %while.165 = (s32[]{:T(128)}, f32[64,64]{1,0:T(8,128)S(1)}, f32[64,64]{1,0:T(8,128)S(1)}, s32[]{:T(128)}, s32[]{:T(128)}, /*index=5*/s32[]{:T(128)}, s32[]{:T(128)}) while((s32[]{:T(128)}, f32[64,64]{1,0:T(8,128)S(1)}, f32[64,64]{1,0:T(8,128)S(1)}, s32[]{:T(128)}, s32[]{:T(128)}, /*index=5*/s32[]{:T(128)}, ...), condition=%wide.region_20.21_spmd.clone.clone, body=%wide.region_18.20_spmd.clone.clone.sunk | while | flops 62086 | bytes 69153 | solution.py:59
  866.7 100.7 %while.158 = (s32[]{:T(128)}, f32[64,64]{0,1:T(8,128)S(1)}, f32[64,64]{0,1:T(8,128)S(1)}, s32[]{:T(128)}) while((s32[]{:T(128)}, f32[64,64]{0,1:T(8,128)S(1)}, f32[64,64]{0,1:T(8,128)S(1)}, s32[]{:T(128)}) %tuple.395), condition=%wide.region_24.25_spmd.clone.clone, body=%wide.region_22.24_spmd.clone.clone.sunk | while | flops 16897 | bytes 69965 | solution.py:78
  967.6 95.1 %while.166 = (s32[]{:T(128)}, f32[64,64]{1,0:T(8,128)S(1)}, f32[64,64]{1,0:T(8,128)S(1)}, s32[]{:T(128)}, s32[]{:T(128)}, /*index=5*/s32[]{:T(128)}, s32[]{:T(128)}) while((s32[]{:T(128)}, f32[64,64]{1,0:T(8,128)S(1)}, f32[64,64]{1,0:T(8,128)S(1)}, s32[]{:T(128)}, s32[]{:T(128)}, /*index=5*/s32[]{:T(128)}, ...), condition=%wide.region_27.28_spmd.clone.clone, body=%wide.region_25.27_spmd.clone.clone.sunk | while | flops 62086 | bytes 69153 | solution.py:59
  1063.3 1.5 convolution_bitcast_fusion.9
  1065.5 103.2 %while.167 = (s32[]{:T(128)}, f32[64,64]{1,0:T(8,128)S(1)}, f32[64,64]{1,0:T(8,128)S(1)}, s32[]{:T(128)}, s32[]{:T(128)}, /*index=5*/s32[]{:T(128)}, s32[]{:T(128)}) while((s32[]{:T(128)}, f32[64,64]{1,0:T(8,128)S(1)}, f32[64,64]{1,0:T(8,128)S(1)}, s32[]{:T(128)}, s32[]{:T(128)}, /*index=5*/s32[]{:T(128)}, ...), condition=%wide.region_31.32_spmd.clone.clone, body=%wide.region_29.31_spmd.clone.clone.sunk | while | flops 62086 | bytes 69153 | solution.py:59
  1066.3 0.8 fusion.236
  1067.9 0.8 fusion.236
  1069.5 0.8 fusion.236
  1087.2 0.8 fusion.236
  1098.5 0.8 fusion.236
  1109.8 0.8 fusion.236
  1111.4 0.8 fusion.236
  1113.0 0.8 fusion.236
  1114.6 0.8 fusion.236
  1116.2 0.8 fusion.236
  1117.8 0.8 fusion.236
  1119.4 0.8 fusion.236
  1140.4 0.8 fusion.236
  1142.0 0.8 fusion.236
  1143.6 0.8 fusion.236
  1150.1 0.8 fusion.236
  1168.9 25.8 %all-reduce.2.cloned.1.call-done = f32[768,64]{0,1:T(8,128)} async-done(((f32[768,64]{0,1:T(8,128)}), f32[768,64]{0,1:T(8,128)}) %all-reduce.2.cloned.1.call-update) | async-done | bytes 196624 | tf_op jit(solution)/shard_map/psum | solution.py:121
  1194.7 1.3 fusion.156
  1196.0 62.1 %all-gather.2.cloned.1.call-done = f32[12288,64]{0,1:T(8,128)} async-done(((f32[384,64]{0,1:T(8,128)}), f32[12288,64]{0,1:T(8,128)}) %all-gather.2.cloned.1.call-update) | async-done | bytes 3145744 | tf_op jit(solution)/shard_map/all_gather | solution.py:114
  1258.1 0.9 constant_dynamic-slice_fusion.8
  1259.4 55.5 %psum.23 = f32[64,64]{1,0:T(8,128)S(1)} all-reduce(f32[64,64]{1,0:T(8,128)S(1)} %fusion.157), channel_id=1, replica_groups=mesh['row'=32,'col'=16] {'col'}, use_global_device_ids=true, to_apply=%region_32.33 | all-reduce | flops 4096 | bytes 32768 | tf_op jit(solution)/shard_map/psum | solution.py:124
  1315.5 2.0 stack.2
  1317.4 10.4 all-to-all-start
  1327.9 124.7 %all-to-all-done = f32[16,768,64]{1,2,0:T(8,128)S(1)} async-done(((f32[16,768,64]{1,2,0:T(8,128)}), f32[16,768,64]{1,2,0:T(8,128)S(1)}, u32[]{:S(2)}, u32[]{:S(2)}) %all-to-all-start) | async-done | bytes 3145760 | tf_op jit(solution)/shard_map/all_to_all | solution.py:128
  1452.9 0.9 copy-done.1
  1453.8 2.2 convolution_subtract_fusion
  (3059 shorter events, 718.7 us)
Async XLA Ops:
  7.2 104.6 %slice-start = ((f32[384,64]{0,1:T(8,128)}), f32[64,64]{0,1:T(8,128)S(1)}, s32[]{:S(2)}) async-start(f32[384,64]{0,1:T(8,128)} %param.23), calls=%async_computation.3 | async-start | bytes 65536 | tf_op jit(solution)/shard_map/slice | solution.py:90
  7.2 1187.5 %all-reduce.2.cloned.1.call-start = ((), (), s32[]{:S(2)}) async-start(), calls=%async_computation.1 | async-start | bytes 393216 | tf_op jit(solution)/shard_map/psum | solution.py:121
  109.8 3.1 collective-permute-start
  214.7 5.8 collective-permute-start.1
  322.3 7.3 collective-permute-start.2
  431.4 5.8 collective-permute-start.3
  539.0 129.0 %collective-permute-start.4 = (f32[64,64]{0,1:T(8,128)S(1)}, f32[64,64]{0,1:T(8,128)S(1)}, u32[]{:S(2)}, u32[]{:S(2)}) collective-permute-start(f32[64,64]{0,1:T(8,128)S(1)} %negate_bitcast_fusion.1), channel_id=1, source_target_pairs={{0,256},{256,0},{16,272},{272,16},{32,288},{288,32},{48,304},{304,... | collective-permute-start | bytes 49160 | tf_op jit(solution)/shard_map/ppermute | solution.py:16
  770.8 291.9 %copy-start.4 = (f32[384,64]{0,1:T(8,128)S(1)}, f32[384,64]{0,1:T(8,128)}, u32[]{:S(2)}) copy-start(f32[384,64]{0,1:T(8,128)} %param.23) | copy-start | bytes 294916
  770.8 292.5 %copy-start = (f32[384,768]{1,0:T(8,128)S(1)}, f32[384,768]{1,0:T(8,128)}, u32[]{:S(2)}) copy-start(f32[384,768]{1,0:T(8,128)} %param.22) | copy-start | bytes 3538948
  865.9 0.6 copy-start.5
  1063.2 1.6 copy-start.2
  1064.8 193.3 %all-gather.2.cloned.1.call-start = ((), (), s32[]{:S(2)}) async-start(), calls=%async_computation.2 | async-start | bytes 3244032 | tf_op jit(solution)/shard_map/all_gather | solution.py:114
  1317.4 135.1 %all-to-all-start = ((f32[16,768,64]{1,2,0:T(8,128)}), f32[16,768,64]{1,2,0:T(8,128)S(1)}, u32[]{:S(2)}, u32[]{:S(2)}) async-start(f32[16,768,64]{1,2,0:T(8,128)} %stack.2), calls=%async_computation | async-start | bytes 6291456 | tf_op jit(solution)/shard_map/all_to_all | solution.py:128
  1452.5 1.3 copy-start.1
  1452.5 1.3 copy-start.3
Sparse Core Ops, SparseCore 0:
  1064.9 129.7 all-reduce.1
  1198.4 59.6 all-gather.1
